TPU v7x, 32 devices: a whole 2x2x4 slice. The times are simulated.
32 devices in a mesh: wide: 8 (over z, y), narrow: 4 (over x, core).
Axes of the slice: x: 2, y: 2, z: 4, core: 2. Of those that a mesh axis runs over, the one named last changes fastest.
Arguments:
- loads: float32 [3, 256, 128, 128], P(None, 'wide', 'narrow'), may hold values from -48 to 48
- targets: float32 [3, 256, 128, 128], P(None, 'wide', 'narrow'), may hold values from -48 to 48
- stiffness: float32 [256, 128, 128], P('wide', 'narrow'), may hold values from 0.5 to 2
- tile_state: int32 [8, 4], P('wide', 'narrow'), may hold values from 0 to 2, as said below
- design_order: int32 [32], replicated, may hold values from 0 to 31, each once
Outputs:
- displacement: float32 [3, 256, 128, 128], P(None, 'wide', 'narrow')
- adjoint: float32 [3, 256, 128, 128], P(None, 'wide', 'narrow')
- design_sens: float32 [32], P(('wide', 'narrow'))
Inputs may be any that keep to these rules, and one draw needn't show every extreme that they name: `tile_state`: 0 marks a tile without rock, 1 rock, 2 weak backfill. `design_order`: each design cell once.
All inputs are finite; a program needn't handle non-finite values.
Results may differ from a plain program's by a relative error of at most 0.0003.
Values sent between devices are 32-bit elements; how exact they have to be, the bound alone decides.
A program may use at most 128 MiB of HBM per device.

v0:
```python
import math

import jax
import jax.numpy as jnp
from jax import lax
from jax.sharding import PartitionSpec as P

DZ = 4
SWEEPS = 3


MASS_SHIFT = 0.5
WEAK_FILL = 0.25
LOW_BOUND = 0.0625
HIGH_BOUND = 34.0
AXES_OF = (0, 0, 1, 1, 2, 2)


def with_halo(cells, sides, width):
    for axis, dim in sides:
        count = lax.axis_size(axis)
        ends = count - 1
        head = lax.slice_in_dim(cells, 0, width, axis=dim)
        tail = lax.slice_in_dim(cells, cells.shape[dim] - width, cells.shape[dim], axis=dim)
        cells = jnp.concatenate(
            [
                lax.ppermute(tail, axis, [(i, (i + 1) % count) for i in range(ends)]),
                cells,
                lax.ppermute(head, axis, [((i + 1) % count, i) for i in range(ends)]),
            ],
            axis=dim,
        )
    return cells


def chebyshev_weights(sweeps):
    center = 0.5 * (HIGH_BOUND + LOW_BOUND)
    spread = 0.5 * (HIGH_BOUND - LOW_BOUND)
    bound_ratio = center / spread
    previous = 1.0 / bound_ratio
    weights = []
    for sweep_index in range(sweeps):
        current = 1.0 / (2.0 * bound_ratio - previous)
        weights.append((current * previous, 2.0 * current / spread))
        previous = current
    return (center, weights)


def axis_gain(axis):
    return jnp.asarray(
        [2.0 if component == axis else 1.0 for component in range(3)], jnp.float32
    ).reshape(3, 1, 1, 1)


def neighbours(padded):
    return [
        padded[..., :-2, 1:-1, 1:-1],
        padded[..., 2:, 1:-1, 1:-1],
        padded[..., 1:-1, :-2, 1:-1],
        padded[..., 1:-1, 2:, 1:-1],
        padded[..., 1:-1, 1:-1, :-2],
        padded[..., 1:-1, 1:-1, 2:],
    ]


def face_terms(stiff_padded):
    center = stiff_padded[1:-1, 1:-1, 1:-1]
    faces = []
    shares = []
    for other in neighbours(stiff_padded):
        present = other > 0.0
        faces.append(jnp.where(present, 0.5 * (center + other), center))
        shares.append(jnp.where(present, 0.5, 1.0).astype(jnp.float32))
    return (faces, shares)


def apply_operator(padded, cell_stiff, active, faces):
    center_field = padded[..., 1:-1, 1:-1, 1:-1]
    total = MASS_SHIFT * cell_stiff * center_field
    for direction, (other, face) in enumerate(zip(neighbours(padded), faces)):
        total = total + axis_gain(AXES_OF[direction]) * face * (center_field - other)
    return active * total


def pad_depth(padded):
    return jnp.pad(padded, [(0, 0)] * (padded.ndim - 1) + [(1, 1)])


def cell_partials(upper, lower, cell_stiff, active, shares):
    center_u = upper[..., 1:-1, 1:-1, 1:-1]
    center_l = lower[..., 1:-1, 1:-1, 1:-1]
    total = MASS_SHIFT * center_u * center_l
    for direction, (other_u, other_l, share) in enumerate(
        zip(neighbours(upper), neighbours(lower), shares)
    ):
        total = total + axis_gain(AXES_OF[direction]) * share * (center_u - other_u) * (
            center_l - other_l
        )
    return -active * cell_stiff * jnp.sum(total, axis=0)


def solve_field(source, exchange_rims, cell_stiff, active, faces):
    center, weights = chebyshev_weights(SWEEPS)
    field = jnp.zeros_like(source)
    residual = source
    direction = source / center
    padded_sum = None
    for sweep_index in range(SWEEPS):
        padded = pad_depth(exchange_rims(direction))
        image = apply_operator(padded, cell_stiff, active, faces)
        field = field + direction
        if sweep_index + 1 < SWEEPS:
            residual = residual - image
            direction = weights[sweep_index][0] * direction + weights[sweep_index][1] * residual
    return (field, padded_sum)


def body(loads, targets, stiffness, tile_state, design_order):
    tiles_x, tiles_y = tile_state.shape
    cells_x = loads.shape[1] // tiles_x
    cells_y = loads.shape[2] // tiles_y
    depth = loads.shape[3]
    factor = jnp.where(tile_state == 1, 1.0, jnp.where(tile_state == 2, WEAK_FILL, 0.0)).astype(
        jnp.float32
    )
    cell_factor = jnp.repeat(jnp.repeat(factor, cells_x, 0), cells_y, 1)[:, :, None]
    cell_stiff = stiffness * cell_factor
    active = (cell_factor > 0.0).astype(jnp.float32)
    stiff_padded = with_halo(cell_stiff, (("wide", 0), ("narrow", 1)), 1)
    stiff_padded = jnp.pad(stiff_padded, ((0, 0), (0, 0), (1, 1)))
    faces, shares = face_terms(stiff_padded)

    def forward_exchange(direction):
        return with_halo(direction, (("wide", 1), ("narrow", 2)), 1)

    def adjoint_exchange(direction):
        return with_halo(direction, (("wide", 1), ("narrow", 2)), 1)

    displacement, upper_sum = solve_field(
        active * loads, forward_exchange, cell_stiff, active, faces
    )
    adjoint, lower_sum = solve_field(active * targets, adjoint_exchange, cell_stiff, active, faces)
    both = with_halo(jnp.stack([displacement, adjoint]), (("wide", 2), ("narrow", 3)), 1)
    both = pad_depth(both)
    upper = both[0]
    lower = both[1]
    partial_value = cell_partials(upper, lower, cell_stiff, active, shares)
    tile_sums = partial_value.reshape(tiles_x, cells_x, tiles_y, cells_y, DZ, depth // DZ).sum(
        axis=(1, 3, 5)
    )
    half_x = tiles_x * lax.axis_size("wide") // 2
    half_y = tiles_y * lax.axis_size("narrow") // 2
    global_x = lax.axis_index("wide") * tiles_x + lax.iota(jnp.int32, tiles_x)
    global_y = lax.axis_index("narrow") * tiles_y + lax.iota(jnp.int32, tiles_y)
    pick_x = (global_x[:, None] // 2 == lax.iota(jnp.int32, half_x)[None, :]).astype(jnp.float32)
    pick_y = (global_y[:, None] // 2 == lax.iota(jnp.int32, half_y)[None, :]).astype(jnp.float32)
    groups = jnp.einsum(
        "ag,bh,abz->ghz", pick_x, pick_y, tile_sums, precision=lax.Precision.HIGHEST
    )
    scale = math.sqrt(4 * cells_x * cells_y * (depth // DZ))
    ordered = groups.reshape(-1)[design_order] / scale
    design_sens = lax.psum_scatter(ordered, ("wide", "narrow"), scatter_dimension=0, tiled=True)
    return (displacement, adjoint, design_sens)


def solution(mesh):
    placed = (
        P(None, "wide", "narrow", None),
        P(None, "wide", "narrow", None),
        P("wide", "narrow", None),
        P("wide", "narrow"),
        P(),
    )
    return jax.shard_map(
        body,
        mesh=mesh,
        in_specs=placed,
        out_specs=(
            P(None, "wide", "narrow", None),
            P(None, "wide", "narrow", None),
            P(("wide", "narrow")),
        ),
        check_vma=False,
    )
```

profile of v0, /device:TPU:0, one launch (start us, length us, event | category | flops | bytes accessed | tf_op | source)
XLA Modules:
  0.0 198.2 jit_solution(18375341838992105784)
XLA Ops:
  1.3 1.9 broadcast_multiply_fusion
  4.0 4.9 %collective-permute-start = (f32[1,32,128]{2,1,0:T(8,128)S(1)}, f32[1,32,128]{2,1,0:T(8,128)S(1)}, u32[]{:S(2)}, u32[]{:S(2)}) collective-permute-start(f32[1,32,128]{2,1,0:T(8,128)S(1)} %get-tuple-element.54), channel_id=1, source_target_pairs={{0,4},{4,8},{8,12},{12,16},{16,20},{20,24},{24,28},{1,5},{5,9},{9,... | collective-permute-start | bytes 49160 | tf_op jit(solution)/shard_map/ppermute | solution.py:27
  10.2 2.3 %multiply_multiply_fusion.24 = (f32[3,32,32,128]{3,2,1,0:T(8,128)S(1)}, f32[3,32,32,128]{3,2,1,0:T(8,128)S(1)}) fusion(f32[3,32,32,128]{3,2,1,0:T(8,128)} %param.36, f32[]{:T(128)S(6)} %convert_element_type.20, f32[3,32,32,128]{3,2,1,0:T(8,128)} %param.35), kind=kLoop, calls=%fused_computation.188 | loop fusion | flops 1572864 | bytes 6291460 | tf_op jit(solution)/shard_map/div | solution.py:106
  12.5 4.5 %collective-permute-start.12 = (f32[3,1,32,128]{3,2,1,0:T(8,128)S(1)}, f32[3,1,32,128]{3,2,1,0:T(8,128)S(1)}, u32[]{:S(2)}, u32[]{:S(2)}) collective-permute-start(f32[3,1,32,128]{3,2,1,0:T(8,128)S(1)} %get-tuple-element.31), channel_id=1, source_target_pairs={{0,4},{4,8},{8,12},{12,16},{16,20},{20,24},{24,28},{1,5},{5,9},{9,... | collective-permute-start | bytes 147464 | tf_op jit(solution)/shard_map/ppermute | solution.py:27
  18.4 5.0 %collective-permute-start.1 = (f32[3,1,32,128]{3,2,1,0:T(8,128)S(1)}, f32[3,1,32,128]{3,2,1,0:T(8,128)S(1)}, u32[]{:S(2)}, u32[]{:S(2)}) collective-permute-start(f32[3,1,32,128]{3,2,1,0:T(8,128)S(1)} %get-tuple-element.35), channel_id=1, source_target_pairs={{0,4},{4,8},{8,12},{12,16},{16,20},{20,24},{24,28},{1,5},{5,9},{9,... | collective-permute-start | bytes 147464 | tf_op jit(solution)/shard_map/ppermute | solution.py:27
  28.4 2.1 %collective-permute-done.6 = f32[34,1,128]{2,1,0:T(1,128)S(1)} collective-permute-done((f32[34,1,128]{2,1,0:T(1,128)S(1)}, f32[34,1,128]{2,1,0:T(1,128)S(1)}, u32[]{:S(2)}, u32[]{:S(2)}) %collective-permute-start.6) | collective-permute-done | bytes 17440 | tf_op jit(solution)/shard_map/ppermute | solution.py:29
  30.6 1.6 select_maximum_fusion.21
  36.1 4.4 %collective-permute-start.14 = (f32[3,34,1,128]{3,2,1,0:T(1,128)S(1)}, f32[3,34,1,128]{3,2,1,0:T(1,128)S(1)}, u32[]{:S(2)}, u32[]{:S(2)}) collective-permute-start(f32[3,34,1,128]{3,2,1,0:T(1,128)S(1)} %get-tuple-element.23), channel_id=1, source_target_pairs={{0,1},{1,2},{2,3},{4,5},{5,6},{6,7},{8,9},{9,10},{10,11},{12,13},{... | collective-permute-start | bytes 156680 | tf_op jit(solution)/shard_map/ppermute | solution.py:27
  42.0 3.0 %collective-permute-start.5 = (f32[3,34,1,128]{3,2,1,0:T(1,128)S(1)}, f32[3,34,1,128]{3,2,1,0:T(1,128)S(1)}, u32[]{:S(2)}, u32[]{:S(2)}) collective-permute-start(f32[3,34,1,128]{3,2,1,0:T(1,128)S(1)} %get-tuple-element.27), channel_id=1, source_target_pairs={{0,1},{1,2},{2,3},{4,5},{5,6},{6,7},{8,9},{9,10},{10,11},{12,13},{... | collective-permute-start | bytes 156680 | tf_op jit(solution)/shard_map/ppermute | solution.py:27
  45.0 1.4 collective-permute-start.7
  46.5 3.6 %select_maximum_fusion.9 = f32[3,34,34,130]{3,2,1,0:T(8,128)S(1)} fusion(f32[3,34,1,128]{3,2,1,0:T(1,128)S(1)} %collective-permute-done.15, f32[3,34,1,128]{3,2,1,0:T(1,128)S(1)} %collective-permute-done.14, f32[3,1,32,128]{3,2,1,0:T(8,128)S(1)} %collective-permute-done.13, f32[3,32,32,128]{3,2,1,0:T(8,128)S(1)} %get-tuple-element.56, ...), kind=kLoop, calls=%fused_computation.17 | loop fusion | flops 5410080 | bytes 3578976 | tf_op jit(solution)/shard_map/concatenate | solution.py:25
  50.2 3.6 %multiply_add_fusion = (f32[3,32,32,128]{3,2,1,0:T(8,128)S(1)}, f32[3,32,32,128]{3,2,1,0:T(8,128)S(1)}) fusion(f32[3,32,32,128]{3,2,1,0:T(8,128)S(1)} %copy-done.5, f32[]{:T(128)S(6)} %convert_element_type.20, f32[3,32,32,128]{3,2,1,0:T(8,128)S(1)} %get-tuple-element.56, f32[3,34,34,130]{3,2,1,0:T(8,128)S(1)} %select_maximum_fusion.9, ...), kind=kLoop, calls=%fused_computation.181 | loop fusion | flops 15335424 | bytes 13309992 | tf_op jit(solution)/shard_map/add | solution.py:114
  53.8 4.9 %collective-permute-start.16 = (f32[3,1,32,128]{3,2,1,0:T(8,128)S(1)}, f32[3,1,32,128]{3,2,1,0:T(8,128)S(1)}, u32[]{:S(2)}, u32[]{:S(2)}) collective-permute-start(f32[3,1,32,128]{3,2,1,0:T(8,128)S(1)} %get-tuple-element.29), channel_id=1, source_target_pairs={{0,4},{4,8},{8,12},{12,16},{16,20},{20,24},{24,28},{1,5},{5,9},{9,... | collective-permute-start | bytes 147464 | tf_op jit(solution)/shard_map/ppermute | solution.py:27
  60.2 3.6 %select_maximum_fusion.17 = f32[3,34,34,130]{3,2,1,0:T(8,128)S(1)} fusion(f32[3,34,1,128]{3,2,1,0:T(1,128)S(1)} %collective-permute-done.7, f32[3,34,1,128]{3,2,1,0:T(1,128)S(1)} %collective-permute-done.5, f32[3,1,32,128]{3,2,1,0:T(8,128)S(1)} %collective-permute-done.3, f32[3,32,32,128]{3,2,1,0:T(8,128)S(1)} %get-tuple-element.57, ...), kind=kLoop, calls=%fused_computation.25 | loop fusion | flops 5410080 | bytes 3578976 | tf_op jit(solution)/shard_map/concatenate | solution.py:25
  63.9 3.6 %multiply_add_fusion.1 = (f32[3,32,32,128]{3,2,1,0:T(8,128)S(1)}, f32[3,32,32,128]{3,2,1,0:T(8,128)S(1)}) fusion(f32[3,32,32,128]{3,2,1,0:T(8,128)S(1)} %copy-done.6, f32[]{:T(128)S(6)} %convert_element_type.20, f32[3,32,32,128]{3,2,1,0:T(8,128)S(1)} %get-tuple-element.57, f32[3,34,34,130]{3,2,1,0:T(8,128)S(1)} %select_maximum_fusion.17, ...), kind=kLoop, calls=%fused_computation.182 | loop fusion | flops 15335424 | bytes 13309992 | tf_op jit(solution)/shard_map/add | solution.py:114
  67.5 5.4 %collective-permute-start.8 = (f32[3,1,32,128]{3,2,1,0:T(8,128)S(1)}, f32[3,1,32,128]{3,2,1,0:T(8,128)S(1)}, u32[]{:S(2)}, u32[]{:S(2)}) collective-permute-start(f32[3,1,32,128]{3,2,1,0:T(8,128)S(1)} %get-tuple-element.33), channel_id=1, source_target_pairs={{0,4},{4,8},{8,12},{12,16},{16,20},{20,24},{24,28},{1,5},{5,9},{9,... | collective-permute-start | bytes 147464 | tf_op jit(solution)/shard_map/ppermute | solution.py:27
  74.4 3.7 %collective-permute-start.18 = (f32[3,34,1,128]{3,2,1,0:T(1,128)S(1)}, f32[3,34,1,128]{3,2,1,0:T(1,128)S(1)}, u32[]{:S(2)}, u32[]{:S(2)}) collective-permute-start(f32[3,34,1,128]{3,2,1,0:T(1,128)S(1)} %get-tuple-element.21), channel_id=1, source_target_pairs={{0,1},{1,2},{2,3},{4,5},{5,6},{6,7},{8,9},{9,10},{10,11},{12,13},{... | collective-permute-start | bytes 156680 | tf_op jit(solution)/shard_map/ppermute | solution.py:27
  79.9 4.4 %collective-permute-start.10 = (f32[3,34,1,128]{3,2,1,0:T(1,128)S(1)}, f32[3,34,1,128]{3,2,1,0:T(1,128)S(1)}, u32[]{:S(2)}, u32[]{:S(2)}) collective-permute-start(f32[3,34,1,128]{3,2,1,0:T(1,128)S(1)} %get-tuple-element.25), channel_id=1, source_target_pairs={{0,1},{1,2},{2,3},{4,5},{5,6},{6,7},{8,9},{9,10},{10,11},{12,13},{... | collective-permute-start | bytes 156680 | tf_op jit(solution)/shard_map/ppermute | solution.py:27
  84.3 1.5 collective-permute-start.11
  85.8 3.6 %select_maximum_fusion.5 = f32[3,34,34,130]{3,2,1,0:T(8,128)S(1)} fusion(f32[3,34,1,128]{3,2,1,0:T(1,128)S(1)} %collective-permute-done.19, f32[3,34,1,128]{3,2,1,0:T(1,128)S(1)} %collective-permute-done.18, f32[3,1,32,128]{3,2,1,0:T(8,128)S(1)} %collective-permute-done.17, f32[3,32,32,128]{3,2,1,0:T(8,128)S(1)} %get-tuple-element.7, ...), kind=kLoop, calls=%fused_computation.13 | loop fusion | flops 5410080 | bytes 3578976 | tf_op jit(solution)/shard_map/concatenate | solution.py:25
  89.5 3.6 %select_maximum_fusion.13 = f32[3,34,34,130]{3,2,1,0:T(8,128)S(1)} fusion(f32[3,34,1,128]{3,2,1,0:T(1,128)S(1)} %collective-permute-done.11, f32[3,34,1,128]{3,2,1,0:T(1,128)S(1)} %collective-permute-done.10, f32[3,1,32,128]{3,2,1,0:T(8,128)S(1)} %collective-permute-done.9, f32[3,32,32,128]{3,2,1,0:T(8,128)S(1)} %get-tuple-element.11, ...), kind=kLoop, calls=%fused_computation.21 | loop fusion | flops 5410080 | bytes 3578976 | tf_op jit(solution)/shard_map/concatenate | solution.py:25
  93.1 3.9 %fusion.39 = f32[3,32,32,128]{3,2,1,0:T(8,128)S(1)} fusion(f32[3,32,32,128]{3,2,1,0:T(8,128)S(1)} %get-tuple-element.8, f32[3,32,32,128]{3,2,1,0:T(8,128)S(1)} %get-tuple-element.7, f32[3,34,34,130]{3,2,1,0:T(8,128)S(1)} %select_maximum_fusion.5, f32[3,34,1,128]{3,2,1,0:T(1,128)S(1)} %collective-permute-done.19, ...), kind=kLoop, calls=%fused_computation.93 | loop fusion | flops 16515072 | bytes 13309992 | tf_op jit(solution)/shard_map/add | solution.py:111
  97.0 3.9 %fusion.20 = f32[3,32,32,128]{3,2,1,0:T(8,128)S(1)} fusion(f32[3,32,32,128]{3,2,1,0:T(8,128)S(1)} %get-tuple-element.12, f32[3,32,32,128]{3,2,1,0:T(8,128)S(1)} %get-tuple-element.11, f32[3,34,34,130]{3,2,1,0:T(8,128)S(1)} %select_maximum_fusion.13, f32[3,34,1,128]{3,2,1,0:T(1,128)S(1)} %collective-permute-done.11, ...), kind=kLoop, calls=%fused_computation.74 | loop fusion | flops 16515072 | bytes 13309992 | tf_op jit(solution)/shard_map/add | solution.py:111
  101.0 5.5 %collective-permute-start.20 = (f32[2,3,1,32,128]{4,3,2,1,0:T(8,128)S(1)}, f32[2,3,1,32,128]{4,3,2,1,0:T(8,128)S(1)}, u32[]{:S(2)}, u32[]{:S(2)}) collective-permute-start(f32[2,3,1,32,128]{4,3,2,1,0:T(8,128)S(1)} %get-tuple-element.17), channel_id=1, source_target_pairs={{0,4},{4,8},{8,12},{12,16},{16,20},{20,24},{24,28},{1,5},{5,9},{9,... | collective-permute-start | bytes 294920 | tf_op jit(solution)/shard_map/ppermute | solution.py:27
  108.6 5.2 %collective-permute-done.21 = f32[2,3,1,32,128]{4,3,2,1,0:T(8,128)S(1)} collective-permute-done((f32[2,3,1,32,128]{4,3,2,1,0:T(8,128)S(1)}, f32[2,3,1,32,128]{4,3,2,1,0:T(8,128)S(1)}, u32[]{:S(2)}, u32[]{:S(2)}) %collective-permute-start.21) | collective-permute-done | bytes 98336 | tf_op jit(solution)/shard_map/ppermute | solution.py:29
  114.0 3.1 %collective-permute-start.22 = (f32[2,3,34,1,128]{4,3,2,1,0:T(1,128)S(1)}, f32[2,3,34,1,128]{4,3,2,1,0:T(1,128)S(1)}, u32[]{:S(2)}, u32[]{:S(2)}) collective-permute-start(f32[2,3,34,1,128]{4,3,2,1,0:T(1,128)S(1)} %get-tuple-element.15), channel_id=1, source_target_pairs={{0,1},{1,2},{2,3},{4,5},{5,6},{6,7},{8,9},{9,10},{10,11},{12,13},{... | collective-permute-start | bytes 313352 | tf_op jit(solution)/shard_map/ppermute | solution.py:27
  117.1 1.5 collective-permute-start.23
  118.7 4.0 %collective-permute-done.23 = f32[2,3,34,1,128]{4,3,2,1,0:T(1,128)S(1)} collective-permute-done((f32[2,3,34,1,128]{4,3,2,1,0:T(1,128)S(1)}, f32[2,3,34,1,128]{4,3,2,1,0:T(1,128)S(1)}, u32[]{:S(2)}, u32[]{:S(2)}) %collective-permute-start.23) | collective-permute-done | bytes 104480 | tf_op jit(solution)/shard_map/ppermute | solution.py:29
  122.7 5.8 %select_maximum_fusion = f32[2,3,34,34,130]{4,3,2,1,0:T(8,128)S(1)} fusion(f32[2,3,34,1,128]{4,3,2,1,0:T(1,128)S(1)} %collective-permute-done.23, f32[2,3,34,1,128]{4,3,2,1,0:T(1,128)S(1)} %collective-permute-done.22, f32[2,3,1,32,128]{4,3,2,1,0:T(8,128)S(1)} %collective-permute-done.21, f32[2,3,1,32,128]{4,3,2,1,0:T(8,128)S(1)} %collective-permute-done.20, ...), kind=kLoop, calls=%fused_computation.3 | loop fusion | flops 12623520 | bytes 7157952 | tf_op jit(solution)/shard_map/concatenate | solution.py:25
  128.5 3.8 %slice_bitcast_fusion.1 = (f32[3,34,34,130]{3,2,1,0:T(8,128)}, f32[3,34,34,130]{3,2,1,0:T(8,128)}) fusion(f32[2,3,34,34,130]{4,3,2,1,0:T(8,128)S(1)} %select_maximum_fusion), kind=kLoop, calls=%fused_computation.12 | loop fusion | bytes 7213440 | tf_op jit(solution)/shard_map/squeeze | solution.py:145
  132.4 20.3 %fusion.42 = f32[32,32,128]{2,1,0:T(8,128)S(1)} fusion(f32[3,34,34,130]{3,2,1,0:T(8,128)} %get-tuple-element.14, f32[3,34,34,130]{3,2,1,0:T(8,128)} %get-tuple-element.13, f32[32,32,128]{2,1,0:T(8,128)S(1)} %copy-done.10, f32[32,32,128]{2,1,0:T(8,128)S(1)} %copy-done.9, f32[32,32,128]{2,1,0:T(8,128)} %get-tuple-element.44, f32[32,32,128]{2,1,0:T(8,128)S(1)} %copy-done.11, ...), kind=kLoop, calls=%fused_computation.97 | loop fusion | flops 15204352 | bytes 25690148 | tf_op jit(solution)/shard_map/reduce_sum | solution.py:99
  153.9 43.7 %all-reduce.6 = f32[32]{0:T(128)S(1)} all-reduce(f32[32]{0:T(128)S(1)} %broadcast_multiply_fusion.4), channel_id=2, replica_groups=mesh['wide'=8,'narrow'=4] {'wide','narrow'}, use_global_device_ids=true, to_apply=%region_3.4.clone | all-reduce | flops 32 | bytes 256
  (93 shorter events, 22.6 us)
Async XLA Ops:
  4.0 19.4 %collective-permute-start = (f32[1,32,128]{2,1,0:T(8,128)S(1)}, f32[1,32,128]{2,1,0:T(8,128)S(1)}, u32[]{:S(2)}, u32[]{:S(2)}) collective-permute-start(f32[1,32,128]{2,1,0:T(8,128)S(1)} %get-tuple-element.54), channel_id=1, source_target_pairs={{0,4},{4,8},{8,12},{12,16},{16,20},{20,24},{24,28},{1,5},{5,9},{9,... | collective-permute-start | bytes 49160 | tf_op jit(solution)/shard_map/ppermute | solution.py:27
  8.9 14.6 %collective-permute-start.2 = (f32[1,32,128]{2,1,0:T(8,128)S(1)}, f32[1,32,128]{2,1,0:T(8,128)S(1)}, u32[]{:S(2)}, u32[]{:S(2)}) collective-permute-start(f32[1,32,128]{2,1,0:T(8,128)S(1)} %get-tuple-element.55), channel_id=1, source_target_pairs={{4,0},{8,4},{12,8},{16,12},{20,16},{24,20},{28,24},{5,1},{9,5},{13... | collective-permute-start | bytes 49160 | tf_op jit(solution)/shard_map/ppermute | solution.py:29
  12.5 23.5 %collective-permute-start.12 = (f32[3,1,32,128]{3,2,1,0:T(8,128)S(1)}, f32[3,1,32,128]{3,2,1,0:T(8,128)S(1)}, u32[]{:S(2)}, u32[]{:S(2)}) collective-permute-start(f32[3,1,32,128]{3,2,1,0:T(8,128)S(1)} %get-tuple-element.31), channel_id=1, source_target_pairs={{0,4},{4,8},{8,12},{12,16},{16,20},{20,24},{24,28},{1,5},{5,9},{9,... | collective-permute-start | bytes 147464 | tf_op jit(solution)/shard_map/ppermute | solution.py:27
  17.1 19.0 %collective-permute-start.13 = (f32[3,1,32,128]{3,2,1,0:T(8,128)S(1)}, f32[3,1,32,128]{3,2,1,0:T(8,128)S(1)}, u32[]{:S(2)}, u32[]{:S(2)}) collective-permute-start(f32[3,1,32,128]{3,2,1,0:T(8,128)S(1)} %get-tuple-element.32), channel_id=1, source_target_pairs={{4,0},{8,4},{12,8},{16,12},{20,16},{24,20},{28,24},{5,1},{9,5},{13... | collective-permute-start | bytes 147464 | tf_op jit(solution)/shard_map/ppermute | solution.py:29
  18.4 23.4 %collective-permute-start.1 = (f32[3,1,32,128]{3,2,1,0:T(8,128)S(1)}, f32[3,1,32,128]{3,2,1,0:T(8,128)S(1)}, u32[]{:S(2)}, u32[]{:S(2)}) collective-permute-start(f32[3,1,32,128]{3,2,1,0:T(8,128)S(1)} %get-tuple-element.35), channel_id=1, source_target_pairs={{0,4},{4,8},{8,12},{12,16},{16,20},{20,24},{24,28},{1,5},{5,9},{9,... | collective-permute-start | bytes 147464 | tf_op jit(solution)/shard_map/ppermute | solution.py:27
  24.5 2.7 %collective-permute-start.4 = (f32[34,1,128]{2,1,0:T(1,128)S(1)}, f32[34,1,128]{2,1,0:T(1,128)S(1)}, u32[]{:S(2)}, u32[]{:S(2)}) collective-permute-start(f32[34,1,128]{2,1,0:T(1,128)S(1)} %get-tuple-element.45), channel_id=1, source_target_pairs={{0,1},{1,2},{2,3},{4,5},{5,6},{6,7},{8,9},{9,10},{10,11},{12,13},{... | collective-permute-start | bytes 52232 | tf_op jit(solution)/shard_map/ppermute | solution.py:27
  25.8 4.8 %collective-permute-start.6 = (f32[34,1,128]{2,1,0:T(1,128)S(1)}, f32[34,1,128]{2,1,0:T(1,128)S(1)}, u32[]{:S(2)}, u32[]{:S(2)}) collective-permute-start(f32[34,1,128]{2,1,0:T(1,128)S(1)} %get-tuple-element.46), channel_id=1, source_target_pairs={{1,0},{2,1},{3,2},{5,4},{6,5},{7,6},{9,8},{10,9},{11,10},{13,12},{... | collective-permute-start | bytes 52232 | tf_op jit(solution)/shard_map/ppermute | solution.py:29
  27.1 14.7 %collective-permute-start.3 = (f32[3,1,32,128]{3,2,1,0:T(8,128)S(1)}, f32[3,1,32,128]{3,2,1,0:T(8,128)S(1)}, u32[]{:S(2)}, u32[]{:S(2)}) collective-permute-start(f32[3,1,32,128]{3,2,1,0:T(8,128)S(1)} %get-tuple-element.36), channel_id=1, source_target_pairs={{4,0},{8,4},{12,8},{16,12},{20,16},{24,20},{28,24},{5,1},{9,5},{13... | collective-permute-start | bytes 147464 | tf_op jit(solution)/shard_map/ppermute | solution.py:29
  36.1 10.3 %collective-permute-start.14 = (f32[3,34,1,128]{3,2,1,0:T(1,128)S(1)}, f32[3,34,1,128]{3,2,1,0:T(1,128)S(1)}, u32[]{:S(2)}, u32[]{:S(2)}) collective-permute-start(f32[3,34,1,128]{3,2,1,0:T(1,128)S(1)} %get-tuple-element.23), channel_id=1, source_target_pairs={{0,1},{1,2},{2,3},{4,5},{5,6},{6,7},{8,9},{9,10},{10,11},{12,13},{... | collective-permute-start | bytes 156680 | tf_op jit(solution)/shard_map/ppermute | solution.py:27
  40.6 5.9 %collective-permute-start.15 = (f32[3,34,1,128]{3,2,1,0:T(1,128)S(1)}, f32[3,34,1,128]{3,2,1,0:T(1,128)S(1)}, u32[]{:S(2)}, u32[]{:S(2)}) collective-permute-start(f32[3,34,1,128]{3,2,1,0:T(1,128)S(1)} %get-tuple-element.24), channel_id=1, source_target_pairs={{1,0},{2,1},{3,2},{5,4},{6,5},{7,6},{9,8},{10,9},{11,10},{13,12},{... | collective-permute-start | bytes 156680 | tf_op jit(solution)/shard_map/ppermute | solution.py:29
  42.0 18.3 %collective-permute-start.5 = (f32[3,34,1,128]{3,2,1,0:T(1,128)S(1)}, f32[3,34,1,128]{3,2,1,0:T(1,128)S(1)}, u32[]{:S(2)}, u32[]{:S(2)}) collective-permute-start(f32[3,34,1,128]{3,2,1,0:T(1,128)S(1)} %get-tuple-element.27), channel_id=1, source_target_pairs={{0,1},{1,2},{2,3},{4,5},{5,6},{6,7},{8,9},{9,10},{10,11},{12,13},{... | collective-permute-start | bytes 156680 | tf_op jit(solution)/shard_map/ppermute | solution.py:27
  45.0 5.1 %copy-start.5 = (f32[3,32,32,128]{3,2,1,0:T(8,128)S(1)}, f32[3,32,32,128]{3,2,1,0:T(8,128)}, u32[]{:S(2)}) copy-start(f32[3,32,32,128]{3,2,1,0:T(8,128)} %param.36) | copy-start | bytes 4718596
  45.0 5.1 %copy-start.12 = (f32[3]{0:T(128)S(1)}, f32[3]{0:T(128)}, u32[]{:S(2)}) copy-start(f32[3]{0:T(128)} %constant.92.clone) | copy-start | bytes 40
  45.0 5.1 %copy-start.13 = (f32[3]{0:T(128)S(1)}, f32[3]{0:T(128)}, u32[]{:S(2)}) copy-start(f32[3]{0:T(128)} %constant.93.clone) | copy-start | bytes 40
  45.0 15.2 %collective-permute-start.7 = (f32[3,34,1,128]{3,2,1,0:T(1,128)S(1)}, f32[3,34,1,128]{3,2,1,0:T(1,128)S(1)}, u32[]{:S(2)}, u32[]{:S(2)}) collective-permute-start(f32[3,34,1,128]{3,2,1,0:T(1,128)S(1)} %get-tuple-element.28), channel_id=1, source_target_pairs={{1,0},{2,1},{3,2},{5,4},{6,5},{7,6},{9,8},{10,9},{11,10},{13,12},{... | collective-permute-start | bytes 156680 | tf_op jit(solution)/shard_map/ppermute | solution.py:29
  53.8 20.5 %collective-permute-start.16 = (f32[3,1,32,128]{3,2,1,0:T(8,128)S(1)}, f32[3,1,32,128]{3,2,1,0:T(8,128)S(1)}, u32[]{:S(2)}, u32[]{:S(2)}) collective-permute-start(f32[3,1,32,128]{3,2,1,0:T(8,128)S(1)} %get-tuple-element.29), channel_id=1, source_target_pairs={{0,4},{4,8},{8,12},{12,16},{16,20},{20,24},{24,28},{1,5},{5,9},{9,... | collective-permute-start | bytes 147464 | tf_op jit(solution)/shard_map/ppermute | solution.py:27
  58.8 15.5 %collective-permute-start.17 = (f32[3,1,32,128]{3,2,1,0:T(8,128)S(1)}, f32[3,1,32,128]{3,2,1,0:T(8,128)S(1)}, u32[]{:S(2)}, u32[]{:S(2)}) collective-permute-start(f32[3,1,32,128]{3,2,1,0:T(8,128)S(1)} %get-tuple-element.30), channel_id=1, source_target_pairs={{4,0},{8,4},{12,8},{16,12},{20,16},{24,20},{28,24},{5,1},{9,5},{13... | collective-permute-start | bytes 147464 | tf_op jit(solution)/shard_map/ppermute | solution.py:29
  67.5 11.9 %collective-permute-start.8 = (f32[3,1,32,128]{3,2,1,0:T(8,128)S(1)}, f32[3,1,32,128]{3,2,1,0:T(8,128)S(1)}, u32[]{:S(2)}, u32[]{:S(2)}) collective-permute-start(f32[3,1,32,128]{3,2,1,0:T(8,128)S(1)} %get-tuple-element.33), channel_id=1, source_target_pairs={{0,4},{4,8},{8,12},{12,16},{16,20},{20,24},{24,28},{1,5},{5,9},{9,... | collective-permute-start | bytes 147464 | tf_op jit(solution)/shard_map/ppermute | solution.py:27
  73.0 6.9 %collective-permute-start.9 = (f32[3,1,32,128]{3,2,1,0:T(8,128)S(1)}, f32[3,1,32,128]{3,2,1,0:T(8,128)S(1)}, u32[]{:S(2)}, u32[]{:S(2)}) collective-permute-start(f32[3,1,32,128]{3,2,1,0:T(8,128)S(1)} %get-tuple-element.34), channel_id=1, source_target_pairs={{4,0},{8,4},{12,8},{16,12},{20,16},{24,20},{28,24},{5,1},{9,5},{13... | collective-permute-start | bytes 147464 | tf_op jit(solution)/shard_map/ppermute | solution.py:29
  74.4 11.4 %collective-permute-start.18 = (f32[3,34,1,128]{3,2,1,0:T(1,128)S(1)}, f32[3,34,1,128]{3,2,1,0:T(1,128)S(1)}, u32[]{:S(2)}, u32[]{:S(2)}) collective-permute-start(f32[3,34,1,128]{3,2,1,0:T(1,128)S(1)} %get-tuple-element.21), channel_id=1, source_target_pairs={{0,1},{1,2},{2,3},{4,5},{5,6},{6,7},{8,9},{9,10},{10,11},{12,13},{... | collective-permute-start | bytes 156680 | tf_op jit(solution)/shard_map/ppermute | solution.py:27
  78.1 7.7 %collective-permute-start.19 = (f32[3,34,1,128]{3,2,1,0:T(1,128)S(1)}, f32[3,34,1,128]{3,2,1,0:T(1,128)S(1)}, u32[]{:S(2)}, u32[]{:S(2)}) collective-permute-start(f32[3,34,1,128]{3,2,1,0:T(1,128)S(1)} %get-tuple-element.22), channel_id=1, source_target_pairs={{1,0},{2,1},{3,2},{5,4},{6,5},{7,6},{9,8},{10,9},{11,10},{13,12},{... | collective-permute-start | bytes 156680 | tf_op jit(solution)/shard_map/ppermute | solution.py:29
  79.9 9.5 %collective-permute-start.10 = (f32[3,34,1,128]{3,2,1,0:T(1,128)S(1)}, f32[3,34,1,128]{3,2,1,0:T(1,128)S(1)}, u32[]{:S(2)}, u32[]{:S(2)}) collective-permute-start(f32[3,34,1,128]{3,2,1,0:T(1,128)S(1)} %get-tuple-element.25), channel_id=1, source_target_pairs={{0,1},{1,2},{2,3},{4,5},{5,6},{6,7},{8,9},{9,10},{10,11},{12,13},{... | collective-permute-start | bytes 156680 | tf_op jit(solution)/shard_map/ppermute | solution.py:27
  84.3 5.1 %collective-permute-start.11 = (f32[3,34,1,128]{3,2,1,0:T(1,128)S(1)}, f32[3,34,1,128]{3,2,1,0:T(1,128)S(1)}, u32[]{:S(2)}, u32[]{:S(2)}) collective-permute-start(f32[3,34,1,128]{3,2,1,0:T(1,128)S(1)} %get-tuple-element.26), channel_id=1, source_target_pairs={{1,0},{2,1},{3,2},{5,4},{6,5},{7,6},{9,8},{10,9},{11,10},{13,12},{... | collective-permute-start | bytes 156680 | tf_op jit(solution)/shard_map/ppermute | solution.py:29
  97.0 25.7 %copy-start = (f32[3,32,32,128]{3,2,1,0:T(8,128)}, f32[3,32,32,128]{3,2,1,0:T(8,128)S(1)}, u32[]{:S(2)}) copy-start(f32[3,32,32,128]{3,2,1,0:T(8,128)S(1)} %fusion.39) | copy-start | bytes 4718596
  100.9 21.8 %copy-start.1 = (f32[3,32,32,128]{3,2,1,0:T(8,128)}, f32[3,32,32,128]{3,2,1,0:T(8,128)S(1)}, u32[]{:S(2)}) copy-start(f32[3,32,32,128]{3,2,1,0:T(8,128)S(1)} %fusion.20) | copy-start | bytes 4718596
  100.9 6.8 %copy-start.16 = (s32[32]{0:T(128)S(1)}, s32[32]{0:T(128)}, u32[]{:S(2)}) copy-start(s32[32]{0:T(128)} %param.39) | copy-start | bytes 388
  101.0 7.7 %collective-permute-start.20 = (f32[2,3,1,32,128]{4,3,2,1,0:T(8,128)S(1)}, f32[2,3,1,32,128]{4,3,2,1,0:T(8,128)S(1)}, u32[]{:S(2)}, u32[]{:S(2)}) collective-permute-start(f32[2,3,1,32,128]{4,3,2,1,0:T(8,128)S(1)} %get-tuple-element.17), channel_id=1, source_target_pairs={{0,4},{4,8},{8,12},{12,16},{16,20},{20,24},{24,28},{1,5},{5,9},{9,... | collective-permute-start | bytes 294920 | tf_op jit(solution)/shard_map/ppermute | solution.py:27
  106.4 7.4 %collective-permute-start.21 = (f32[2,3,1,32,128]{4,3,2,1,0:T(8,128)S(1)}, f32[2,3,1,32,128]{4,3,2,1,0:T(8,128)S(1)}, u32[]{:S(2)}, u32[]{:S(2)}) collective-permute-start(f32[2,3,1,32,128]{4,3,2,1,0:T(8,128)S(1)} %get-tuple-element.18), channel_id=1, source_target_pairs={{4,0},{8,4},{12,8},{16,12},{20,16},{24,20},{28,24},{5,1},{9,5},{13... | collective-permute-start | bytes 294920 | tf_op jit(solution)/shard_map/ppermute | solution.py:29
  108.2 10.4 %copy-start.15 = (s32[32]{0:T(128)S(1)}, s32[32]{0:T(128)}, u32[]{:S(2)}) copy-start(s32[32]{0:T(128)} %compare_select_fusion) | copy-start | bytes 388
  114.0 4.7 %collective-permute-start.22 = (f32[2,3,34,1,128]{4,3,2,1,0:T(1,128)S(1)}, f32[2,3,34,1,128]{4,3,2,1,0:T(1,128)S(1)}, u32[]{:S(2)}, u32[]{:S(2)}) collective-permute-start(f32[2,3,34,1,128]{4,3,2,1,0:T(1,128)S(1)} %get-tuple-element.15), channel_id=1, source_target_pairs={{0,1},{1,2},{2,3},{4,5},{5,6},{6,7},{8,9},{9,10},{10,11},{12,13},{... | collective-permute-start | bytes 313352 | tf_op jit(solution)/shard_map/ppermute | solution.py:27
  117.1 5.6 %collective-permute-start.23 = (f32[2,3,34,1,128]{4,3,2,1,0:T(1,128)S(1)}, f32[2,3,34,1,128]{4,3,2,1,0:T(1,128)S(1)}, u32[]{:S(2)}, u32[]{:S(2)}) collective-permute-start(f32[2,3,34,1,128]{4,3,2,1,0:T(1,128)S(1)} %get-tuple-element.16), channel_id=1, source_target_pairs={{1,0},{2,1},{3,2},{5,4},{6,5},{7,6},{9,8},{10,9},{11,10},{13,12},{... | collective-permute-start | bytes 313352 | tf_op jit(solution)/shard_map/ppermute | solution.py:29
  132.4 20.3 %copy-start.4 = (f32[32,32,128]{2,1,0:T(8,128)S(1)}, f32[32,32,128]{2,1,0:T(8,128)}, u32[]{:S(2)}) copy-start(f32[32,32,128]{2,1,0:T(8,128)} %copy-done.2) | copy-start | bytes 1572868
  (9 other events, 31.3 us)
where the time goes:
time: 199 us; the launch traced here: 198 us
  other arithmetic  67.7 us (34%)
  starting transfers between devices  66.3 us (33%)
  blocking collectives  43.7 us (22%)
  waiting for transfers between devices  12.3 us (6%)
  local copies, waits for them, and re-layouts  6.22 us (3%)
  between operations  2.04 us (1%)
    ppermute x12, starting transfers between devices, with_halo(): lax.ppermute(tail, axis, [(i, (i + 1) % count) for i in range(ends)])  50.1 us
    unnamed x1, blocking collectives  43.7 us
    concatenate x6, other arithmetic, with_halo(): jnp.concatenate([lax.ppermute(tail, axis, [(i, (i + 1) % count) for i in...  21.8 us
    reduce_sum x1, other arithmetic, cell_partials(): return -active * cell_stiff * jnp.sum(total, axis=0)  20.3 us
    ppermute x12, starting transfers between devices, with_halo(): lax.ppermute(head, axis, [((i + 1) % count, i) for i in range(ends)])  16.2 us
    ppermute x12, waiting for transfers between devices, with_halo(): lax.ppermute(head, axis, [((i + 1) % count, i) for i in range(ends)])  11.9 us
    add x2, other arithmetic, solve_field(): field = field + direction  7.75 us
    add x2, other arithmetic, solve_field(): weights[sweep_index][0] * direction + weights[sweep_index][1] * residual  7.28 us
  transfers between devices with their start and end apart: 24, of which 5 were waited for; matrix products, arithmetic and copies ran while one was open for 14% of the time, Pallas kernels for 0%

commit v1 on v0

v1 whole, which is shorter than its diff:
```python
import functools
import math

import jax
import jax.numpy as jnp
from jax import lax
from jax.experimental import pallas as pl
from jax.experimental.pallas import tpu as pltpu
from jax.sharding import PartitionSpec as P

DZ = 4
SWEEPS = 3
WEAK_FILL = 0.25
LOW_BOUND = 0.0625
HIGH_BOUND = 34.0
F32 = jnp.float32


def chebyshev_weights(sweeps):
    center = 0.5 * (HIGH_BOUND + LOW_BOUND)
    spread = 0.5 * (HIGH_BOUND - LOW_BOUND)
    bound_ratio = center / spread
    previous = 1.0 / bound_ratio
    weights = []
    for sweep_index in range(sweeps):
        current = 1.0 / (2.0 * bound_ratio - previous)
        weights.append((current * previous, 2.0 * current / spread))
        previous = current
    return (center, weights)


def sweep_constants():
    center, weights = chebyshev_weights(SWEEPS)
    (w00, w01), (w10, w11) = weights[0], weights[1]
    alpha = w00 / center + w01
    beta = w01 / center
    p = 1.0 / center - w11 * w00 / (w01 * center)
    q = 1.0 + w10 + w11 / w01
    return alpha, beta, p, q, w11


def kernel(
    nw, nn, loads, targets, stiff, state, order, u_out, l_out, sens,
    s, d, kh, fac_own, fac_in, ys_out, ys_in, yd_out, yd_in, yx_out, yx_in,
    tile_a, send_a, tile_b, send_b,
    in_sem, out_sem, xs_send, xs_recv, ys_send, ys_recv, xd_send, xd_recv,
    yd_send, yd_recv, xx_send, xx_recv, a_send, a_recv, b_send, b_recv,
):
    cells_x, cells_y, depth = stiff.shape
    last = cells_x + 1
    w = lax.axis_index("wide")
    n = lax.axis_index("narrow")
    has_x = (w > 0, w < nw - 1)
    has_y = (n > 0, n < nn - 1)
    steps = (-1, 1)

    def at(wi, ni):
        return dict(device_id=(wi, ni), device_id_type=pl.DeviceIdType.MESH)

    def x_peer(side):
        return at(w + steps[side], n)

    def y_peer(side):
        return at(w, n + steps[side])

    barrier = pltpu.get_barrier_semaphore()
    for m in range(nn):
        @pl.when(m != n)
        def _():
            pl.semaphore_signal(barrier, inc=1, **at(w, jnp.int32(m)))
    for m in range(nw):
        @pl.when(m != w)
        def _():
            pl.semaphore_signal(barrier, inc=1, **at(jnp.int32(m), n))

    local = [
        pltpu.make_async_copy(stiff, kh.at[pl.ds(1, cells_x)], in_sem.at[0]),
        pltpu.make_async_copy(loads, s.at[pl.ds(0, 3), pl.ds(1, cells_x)], in_sem.at[1]),
        pltpu.make_async_copy(targets, s.at[pl.ds(3, 3), pl.ds(1, cells_x)], in_sem.at[2]),
    ]
    for copy in local:
        copy.start()

    own_state = state[0, 0]
    factor = jnp.where(own_state == 1, 1.0, jnp.where(own_state == 2, WEAK_FILL, 0.0)).astype(F32)
    act = jnp.where(factor > 0.0, 1.0, 0.0).astype(F32)
    fac_own[...] = jnp.full(fac_own.shape, factor, F32)

    pl.semaphore_wait(barrier, nn - 1 + nw - 1)

    edge = (0, cells_x - 1)
    ghost = (0, last)

    def xs_copies(side):
        there = 1 - side
        pairs = (
            (stiff.at[edge[side]], kh.at[ghost[there]]),
            (loads.at[:, edge[side]], s.at[pl.ds(0, 3), ghost[there]]),
            (targets.at[:, edge[side]], s.at[pl.ds(3, 3), ghost[there]]),
            (fac_own, fac_in.at[there]),
        )
        return [
            pltpu.make_async_remote_copy(
                src_ref=a, dst_ref=b, send_sem=xs_send.at[side, t], recv_sem=xs_recv.at[there, t],
                **x_peer(side))
            for t, (a, b) in enumerate(pairs)
        ]

    def one(src, dst, sends, recvs, side, peer):
        return pltpu.make_async_remote_copy(
            src_ref=src, dst_ref=dst, send_sem=sends.at[side], recv_sem=recvs.at[1 - side],
            **peer(side))

    def ys_copy(side):
        return one(ys_out.at[side], ys_in.at[1 - side], ys_send, ys_recv, side, y_peer)

    def yd_copy(side):
        return one(yd_out.at[side], yd_in.at[1 - side], yd_send, yd_recv, side, y_peer)

    def xd_copy(side):
        return one(d.at[:, 1 + edge[side]], d.at[:, ghost[1 - side]], xd_send, xd_recv, side, x_peer)

    def xx_copy():
        return pltpu.make_async_remote_copy(
            src_ref=s.at[:, cells_x], dst_ref=s.at[:, 0], send_sem=xx_send.at[0],
            recv_sem=xx_recv.at[0], **x_peer(1))

    def yx_copy():
        return pltpu.make_async_remote_copy(
            src_ref=yx_out, dst_ref=yx_in, send_sem=xx_send.at[1],
            recv_sem=xx_recv.at[1], **y_peer(1))

    for side in (0, 1):
        @pl.when(has_x[side])
        def _():
            for copy in xs_copies(side):
                copy.start()

        @pl.when(jnp.logical_not(has_x[side]))
        def _():
            s[:, ghost[side]] = jnp.zeros((6, cells_y, depth), F32)
            d[:, ghost[side]] = jnp.zeros((6, cells_y, depth), F32)
            fac_in[side] = jnp.zeros(fac_in.shape[1:], F32)

        @pl.when(jnp.logical_not(has_y[side]))
        def _():
            ys_in[side] = jnp.zeros(ys_in.shape[1:], F32)
            yd_in[side] = jnp.zeros(yd_in.shape[1:], F32)

    @pl.when(n == 0)
    def _():
        yx_in[...] = jnp.zeros(yx_in.shape, F32)

    for copy in local:
        copy.wait()

    half_factor = 0.5 * factor
    y_edge = (slice(0, 1), slice(cells_y - 1, cells_y))

    def prepare(t, carry):
        plane = kh[t + 1] * half_factor
        kh[t + 1] = plane
        for side in (0, 1):
            ys_out[side, 6, pl.ds(t, 1)] = plane[y_edge[side]]
            for c in range(6):
                ys_out[side, c, pl.ds(t, 1)] = s[c, t + 1, y_edge[side]] * act
        return carry

    lax.fori_loop(0, cells_x, prepare, 0)

    for side in (0, 1):
        @pl.when(has_y[side])
        def _():
            ys_copy(side).start()

    for side in (0, 1):
        @pl.when(has_y[side])
        def _():
            ys_copy(1 - side).wait_recv()

    row = lax.broadcasted_iota(jnp.int32, (cells_y, depth), 0)
    lane = lax.broadcasted_iota(jnp.int32, (cells_y, depth), 1)
    first_row, last_row = row == 0, row == cells_y - 1
    first_lane, last_lane = lane == 0, lane == depth - 1

    def down(v, halo):
        return jnp.where(first_row, halo, pltpu.roll(v, 1, 0))

    def up(v, halo):
        return jnp.where(last_row, halo, pltpu.roll(v, cells_y - 1, 0))

    def left(v):
        return pltpu.roll(v, 1, 1)

    def right(v):
        return pltpu.roll(v, depth - 1, 1)

    def y_stiff(kc, side, t):
        halo = ys_in[side, 6, pl.ds(t, 1)]
        return jnp.where(halo > 0.0, halo, kc[y_edge[side]])

    def operator(src, y_in, i, emit):
        t = i - 1
        kc = kh[i]
        fxm, fxp = kc + kh[i - 1], kc + kh[i + 1]
        fym = kc + down(kc, y_stiff(kc, 0, t))
        fyp = kc + up(kc, y_stiff(kc, 1, t))
        fzm = kc + jnp.where(first_lane, kc, left(kc))
        fzp = kc + jnp.where(last_lane, kc, right(kc))
        sums = (fxm + fxp, fym + fyp, fzm + fzp)
        total = kc + (sums[0] + sums[1] + sums[2])
        diag = [total + part for part in sums]
        fzm = jnp.where(first_lane, 0.0, fzm)
        fzp = jnp.where(last_lane, 0.0, fzp)
        for c in range(6):
            v = src[c, i]
            ax = fxm * src[c, i - 1] + fxp * src[c, i + 1]
            ay = fym * down(v, y_in[0, c, pl.ds(t, 1)]) + fyp * up(v, y_in[1, c, pl.ds(t, 1)])
            az = fzm * left(v) + fzp * right(v)
            mine = (ax, ay, az)[c % 3]
            emit(c, i, v, diag[c % 3] * v - ((ax + ay) + (az + mine)))

    alpha, beta, p, q, wd = sweep_constants()
    alpha_a, beta_a, p_a, wd_a = alpha * act, beta * act, p * act, wd * act

    def emit_d(c, i, v, image):
        plane = alpha_a * v - beta_a * image
        d[c, i] = plane
        for side in (0, 1):
            yd_out[side, c, pl.ds(i - 1, 1)] = plane[y_edge[side]]

    def emit_x(c, i, v, image):
        plane = p_a * s[c, i] + (q * v - wd_a * image)
        s[c, i] = plane
        yx_out[c, pl.ds(i - 1, 1)] = plane[y_edge[1]]

    def first_pass(i, carry):
        operator(s, ys_in, i, emit_d)
        return carry

    def second_pass(i, carry):
        operator(d, yd_in, i, emit_x)
        return carry

    lax.fori_loop(2, cells_x, first_pass, 0)

    for side in (0, 1):
        @pl.when(has_x[side])
        def _():
            for copy in xs_copies(1 - side):
                copy.wait_recv()
        theirs = fac_in[side][0:1]
        present = theirs > 0.0
        inner = kh[1 + edge[side]]

        @pl.when(has_x[side])
        def _():
            kh[ghost[side]] = jnp.where(present, kh[ghost[side]] * (0.5 * theirs), inner)
            for c in range(6):
                s[c, ghost[side]] = jnp.where(present, s[c, ghost[side]], 0.0)

        @pl.when(jnp.logical_not(has_x[side]))
        def _():
            kh[ghost[side]] = inner

    lax.fori_loop(0, 2, lambda t, c: first_pass(1 + t * (cells_x - 1), c), 0)

    for side in (0, 1):
        @pl.when(has_x[side])
        def _():
            xd_copy(side).start()

    for side in (0, 1):
        @pl.when(has_y[side])
        def _():
            yd_copy(side).start()

    for side in (0, 1):
        @pl.when(has_y[side])
        def _():
            yd_copy(1 - side).wait_recv()

    lax.fori_loop(2, cells_x, second_pass, 0)

    for side in (0, 1):
        @pl.when(has_x[side])
        def _():
            xd_copy(1 - side).wait_recv()

    lax.fori_loop(0, 2, lambda t, c: second_pass(1 + (1 - t) * (cells_x - 1), c), 0)

    @pl.when(has_x[1])
    def _():
        xx_copy().start()

    @pl.when(has_y[1])
    def _():
        yx_copy().start()

    results = [
        pltpu.make_async_copy(s.at[pl.ds(0, 3), pl.ds(1, cells_x)], u_out, out_sem.at[0]),
        pltpu.make_async_copy(s.at[pl.ds(3, 3), pl.ds(1, cells_x)], l_out, out_sem.at[1]),
    ]
    for copy in results:
        copy.start()

    @pl.when(has_y[0])
    def _():
        yx_copy().wait_recv()

    other_share = jnp.where(factor > 0.0, 1.0, 2.0).astype(F32)
    end_x = jnp.where(w == nw - 1, 2.0, 0.0).astype(F32)
    end_y = jnp.where(n == nn - 1, 2.0, 0.0).astype(F32)
    zero_plane = jnp.zeros((cells_y, depth), F32)
    zero_row = jnp.zeros((1, depth), F32)

    def products(shift, axis):
        total = None
        for c in range(3):
            (u, un), (l, ln) = shift(c), shift(c + 3)
            term = (u - un) * (l - ln)
            if c == axis:
                term = term + term
            total = term if total is None else total + term
        return total

    def face_sums(t, carry, behind=True):
        own, back, below = carry
        i = t + 1
        kc = kh[i]
        fields = [s[c, i] for c in range(6)]
        squares = [fields[c] * fields[c + 3] for c in range(3)]
        mass = squares[0] + squares[1] + squares[2]
        far_x = jnp.where(t == cells_x - 1, end_x, 0.0)
        far_y = jnp.where(last_row, end_y, 0.0)
        far_z = jnp.where(last_lane, 2.0, 0.0)
        own = own + kc * (
            mass + far_x * (mass + squares[0]) + far_y * (mass + squares[1])
            + far_z * (mass + squares[2]))
        if behind:
            px = products(lambda c: (fields[c], s[c, i - 1]), 0)
            own = own + (kc + kh[i - 1]) * px
        halo = ys_in[0, 6, pl.ds(t, 1)]
        py = products(lambda c: (fields[c], down(fields[c], yx_in[c, pl.ds(t, 1)])), 1)
        edge_weight = jnp.where(halo > 0.0, 0.0, kc[0:1])
        own = own + (kc + down(kc, edge_weight)) * py
        below = below + (other_share * halo) * py[0:1]
        pz = products(lambda c: (fields[c], jnp.where(first_lane, 0.0, left(fields[c]))), 2)
        own = own + jnp.where(first_lane, kc + kc, kc) * pz
        back = back + jnp.where(first_lane, 0.0, left(kc)) * pz
        return own, back, below

    start = face_sums(0, (zero_plane, zero_plane, zero_row), behind=False)
    own, back, below = lax.fori_loop(1, cells_x, face_sums, start)

    @pl.when(has_x[0])
    def _():
        xx_copy().wait_recv()

    px = products(lambda c: (s[c, 1], s[c, 0]), 0)
    present = fac_in[0][0:1] > 0.0
    own = own + kh[1] * jnp.where(present, 1.0, 2.0) * px
    beside = jnp.where(present, other_share * kh[0], 0.0) * px

    def fold(v):
        return jnp.sum(v, axis=0, keepdims=True)

    own_row = fold(own) + right(jnp.broadcast_to(fold(back), (8, depth)))[0:1]
    send_a[...] = jnp.concatenate(
        [own_row, fold(beside), below, jnp.zeros((5, depth), F32)], axis=0)

    def a_copy(m, slot):
        return pltpu.make_async_remote_copy(
            src_ref=send_a, dst_ref=tile_a.at[slot], send_sem=a_send.at[m],
            recv_sem=a_recv.at[slot], **at(w, jnp.int32(m)))

    def b_copy(m, slot):
        return pltpu.make_async_remote_copy(
            src_ref=send_b, dst_ref=tile_b.at[slot], send_sem=b_send.at[m],
            recv_sem=b_recv.at[slot], **at(jnp.int32(m), n))

    for m in range(nn):
        @pl.when(m != n)
        def _():
            a_copy(m, n).start()
    tile_a[n] = send_a[...]
    for m in range(nn):
        @pl.when(m != n)
        def _():
            a_copy(m, m).wait_recv()

    groups_y = nn // 2
    rows = [zero_row] * (2 * groups_y)
    for m in range(nn):
        tile = tile_a[m]
        rows[m // 2] = rows[m // 2] + tile[0:1]
        rows[groups_y + m // 2] = rows[groups_y + m // 2] + tile[1:2]
        if m > 0:
            rows[(m - 1) // 2] = rows[(m - 1) // 2] + tile[2:3]
    high = send_b.shape[0]
    if high > len(rows):
        rows.append(jnp.zeros((high - len(rows), depth), F32))
    send_b[...] = jnp.concatenate(rows, axis=0)

    for m in range(nw):
        @pl.when(m != w)
        def _():
            b_copy(m, w).start()
    tile_b[w] = send_b[...]
    for m in range(nw):
        @pl.when(m != w)
        def _():
            b_copy(m, m).wait_recv()

    wanted = order[w * nn + n]
    b_row = lax.broadcasted_iota(jnp.int32, (high, depth), 0)
    b_block = lax.broadcasted_iota(jnp.int32, (high, depth), 1) // (depth // DZ)
    picked = jnp.zeros((high, depth), F32)
    for m in range(nw):
        near = ((m // 2) * groups_y + b_row) * DZ + b_block
        far = (((m - 1) // 2) * groups_y + b_row - groups_y) * DZ + b_block if m > 0 else -1
        index = jnp.where(b_row < groups_y, near, far)
        index = jnp.where(b_row < 2 * groups_y, index, -1)
        picked = picked + jnp.where(index == wanted, tile_b[m], 0.0)
    scale = math.sqrt(4 * cells_x * cells_y * (depth // DZ))
    sens[0] = jnp.sum(picked) * (-1.0 / scale)

    for copy in results:
        copy.wait()
    for side in (0, 1):
        @pl.when(has_x[side])
        def _():
            for copy in xs_copies(side):
                copy.wait_send()
            xd_copy(side).wait_send()

        @pl.when(has_y[side])
        def _():
            ys_copy(side).wait_send()
            yd_copy(side).wait_send()

    @pl.when(has_x[1])
    def _():
        xx_copy().wait_send()

    @pl.when(has_y[1])
    def _():
        yx_copy().wait_send()

    for m in range(nn):
        @pl.when(m != n)
        def _():
            a_copy(m, n).wait_send()
    for m in range(nw):
        @pl.when(m != w)
        def _():
            b_copy(m, w).wait_send()


def body(nw, nn, loads, targets, stiffness, tile_state, design_order):
    cells_x, cells_y, depth = stiffness.shape
    high = -(-nn // 8) * 8
    dma = pltpu.SemaphoreType.DMA
    vmem = pltpu.VMEM
    anywhere = pl.BlockSpec(memory_space=pl.ANY)
    smem = pl.BlockSpec(memory_space=pltpu.SMEM)
    field = (6, cells_x + 2, cells_y, depth)
    return pl.pallas_call(
        functools.partial(kernel, nw, nn),
        out_shape=(
            jax.ShapeDtypeStruct(loads.shape, F32),
            jax.ShapeDtypeStruct(targets.shape, F32),
            jax.ShapeDtypeStruct((1,), F32),
        ),
        in_specs=[anywhere, anywhere, anywhere, smem, smem],
        out_specs=(anywhere, anywhere, smem),
        scratch_shapes=[
            vmem(field, F32),
            vmem(field, F32),
            vmem(field[1:], F32),
            vmem((8, depth), F32),
            vmem((2, 8, depth), F32),
            vmem((2, 7, cells_x, depth), F32),
            vmem((2, 7, cells_x, depth), F32),
            vmem((2, 6, cells_x, depth), F32),
            vmem((2, 6, cells_x, depth), F32),
            vmem((6, cells_x, depth), F32),
            vmem((6, cells_x, depth), F32),
            vmem((nn, 8, depth), F32),
            vmem((8, depth), F32),
            vmem((nw, high, depth), F32),
            vmem((high, depth), F32),
            dma((3,)),
            dma((2,)),
            dma((2, 4)),
            dma((2, 4)),
            dma((2,)),
            dma((2,)),
            dma((2,)),
            dma((2,)),
            dma((2,)),
            dma((2,)),
            dma((2,)),
            dma((2,)),
            dma((nn,)),
            dma((nn,)),
            dma((nw,)),
            dma((nw,)),
        ],
        compiler_params=pltpu.CompilerParams(
            collective_id=0, has_side_effects=True, vmem_limit_bytes=40 * 1024 * 1024
        ),
    )(loads, targets, stiffness, tile_state, design_order)


def solution(mesh):
    placed = (
        P(None, "wide", "narrow", None),
        P(None, "wide", "narrow", None),
        P("wide", "narrow", None),
        P("wide", "narrow"),
        P(),
    )
    return jax.shard_map(
        functools.partial(body, mesh.shape["wide"], mesh.shape["narrow"]),
        mesh=mesh,
        in_specs=placed,
        out_specs=(
            P(None, "wide", "narrow", None),
            P(None, "wide", "narrow", None),
            P(("wide", "narrow")),
        ),
        check_vma=False,
    )
```

time: 199 us -> 45.6 us (0.23)
  other arithmetic: 67.7 us -> 0 us
  starting transfers between devices: 66.3 us -> 0 us
  blocking collectives: 43.7 us -> 0 us
  Pallas kernels: 0 us -> 35.5 us
  waiting for transfers between devices: 12.3 us -> 0 us
    ppermute x24 -> x0, starting transfers between devices: 66.3 us -> none  [the longest x12 50.1 us: with_halo(): lax.ppermute(tail, axis, [(i, (i + 1) % count) for i in range(ends)])]
    unnamed x1 -> x0, blocking collectives: 43.7 us -> none
    pallas_call x0 -> x1, Pallas kernels: none -> 35.5 us  [body(): pl.pallas_call(functools.partial(kernel, nw, nn), out_shape=(jax.ShapeDty...]
    concatenate x6 -> x0, other arithmetic: 21.8 us -> none  [with_halo(): jnp.concatenate([lax.ppermute(tail, axis, [(i, (i + 1) % count) for i in...]
    reduce_sum x3 -> x0, other arithmetic: 20.6 us -> none  [the longest x1 20.3 us: cell_partials(): return -active * cell_stiff * jnp.sum(total, axis=0)]
    add x4 -> x0, other arithmetic: 15 us -> none  [the longest x2 7.75 us: solve_field(): field = field + direction]
    ppermute x24 -> x0, waiting for transfers between devices: 12.3 us -> none  [the longest x12 11.9 us: with_halo(): lax.ppermute(head, axis, [((i + 1) % count, i) for i in range(ends)])]
    unnamed x35 -> x10, local copies, waits for them, and re-layouts: 1.48 us -> 6.79 us
  transfers between devices with their start and end apart: 24 -> 0, of which waited for: 5 -> 0; matrix products, arithmetic and copies ran while one was open for 14% -> 0% of each run, Pallas kernels for 0% -> 0%
where the time goes in v1:
time: 45.6 us; the launch traced here: 45.4 us
  Pallas kernels  35.5 us (78%)
  local copies, waits for them, and re-layouts  6.79 us (15%)
  between operations  3.05 us (7%)
    pallas_call x1, Pallas kernels, body(): pl.pallas_call(functools.partial(kernel, nw, nn), out_shape=(jax.ShapeDty...  35.5 us
    unnamed x10, local copies, waits for them, and re-layouts  6.79 us

profile of v1, /device:TPU:0, one launch (start us, length us, event | category | flops | bytes accessed | tf_op | source)
XLA Modules:
  0.0 45.4 jit_solution(15801851827002424420)
XLA Ops:
  1.3 0.0 copy-start
  1.3 1.4 %copy-done = f32[3,32,32,128]{3,2,1,0:T(8,128)S(1)} copy-done((f32[3,32,32,128]{3,2,1,0:T(8,128)S(1)}, f32[3,32,32,128]{3,2,1,0:T(8,128)}, u32[]{:S(2)}) %copy-start) | copy-done | bytes 1572888
  2.7 0.0 copy-start.1
  2.7 1.4 %copy-done.1 = f32[3,32,32,128]{3,2,1,0:T(8,128)S(1)} copy-done((f32[3,32,32,128]{3,2,1,0:T(8,128)S(1)}, f32[3,32,32,128]{3,2,1,0:T(8,128)}, u32[]{:S(2)}) %copy-start.1) | copy-done | bytes 1572888
  4.1 0.0 copy-start.2
  4.1 1.0 %copy-done.2 = f32[32,32,128]{2,1,0:T(8,128)S(1)} copy-done((f32[32,32,128]{2,1,0:T(8,128)S(1)}, f32[32,32,128]{2,1,0:T(8,128)}, u32[]{:S(2)}) %copy-start.2) | copy-done | bytes 524312
  5.1 0.0 copy-start.3
  5.1 0.7 %copy-done.3 = s32[32]{0:T(128)S(1)} copy-done((s32[32]{0:T(128)S(1)}, s32[32]{0:T(128)}, u32[]{:S(2)}) %copy-start.3) | copy-done | bytes 152
  5.8 35.5 %shard_map.76 = (f32[3,32,32,128]{3,2,1,0:T(8,128)S(1)}, f32[3,32,32,128]{3,2,1,0:T(8,128)S(1)}, f32[1]{0:T(128)}) custom-call(f32[3,32,32,128]{3,2,1,0:T(8,128)S(1)} %copy-done, f32[3,32,32,128]{3,2,1,0:T(8,128)S(1)} %copy-done.1, f32[32,32,128]{2,1,0:T(8,128)S(1)} %copy-done.2, s32[1,1]{1,0:T(1,128)S(6)} %copy.11.state, s32[32]{0:T(128)S(1)} %copy-done.3), custom_call_target="tpu_custom_call" | custom-call | tf_op jit(solution)/shard_map/pallas_call | solution.py:468
  41.3 1.1 %copy.12 = f32[3,32,32,128]{3,2,1,0:T(8,128)} copy(f32[3,32,32,128]{3,2,1,0:T(8,128)S(1)} %get-tuple-element.6) | data formatting | bytes 3145728
  42.5 1.1 %copy.13 = f32[3,32,32,128]{3,2,1,0:T(8,128)} copy(f32[3,32,32,128]{3,2,1,0:T(8,128)S(1)} %get-tuple-element.7) | data formatting | bytes 3145728
Async XLA Ops:
  1.3 1.4 %copy-start = (f32[3,32,32,128]{3,2,1,0:T(8,128)S(1)}, f32[3,32,32,128]{3,2,1,0:T(8,128)}, u32[]{:S(2)}) copy-start(f32[3,32,32,128]{3,2,1,0:T(8,128)} %loads.1) | copy-start | bytes 4718596
  2.7 1.4 %copy-start.1 = (f32[3,32,32,128]{3,2,1,0:T(8,128)S(1)}, f32[3,32,32,128]{3,2,1,0:T(8,128)}, u32[]{:S(2)}) copy-start(f32[3,32,32,128]{3,2,1,0:T(8,128)} %targets.1) | copy-start | bytes 4718596
  4.1 1.0 %copy-start.2 = (f32[32,32,128]{2,1,0:T(8,128)S(1)}, f32[32,32,128]{2,1,0:T(8,128)}, u32[]{:S(2)}) copy-start(f32[32,32,128]{2,1,0:T(8,128)} %stiff.1) | copy-start | bytes 1572868
  5.1 0.7 %copy-start.3 = (s32[32]{0:T(128)S(1)}, s32[32]{0:T(128)}, u32[]{:S(2)}) copy-start(s32[32]{0:T(128)} %order.1) | copy-start | bytes 388

commit v2 on v1

--- a/solution.py
+++ b/solution.py
@@ -40,11 +40,11 @@
 
 
 def kernel(
-    nw, nn, loads, targets, stiff, state, order, u_out, l_out, sens,
-    s, d, kh, fac_own, fac_in, ys_out, ys_in, yd_out, yd_in, yx_out, yx_in,
-    tile_a, send_a, tile_b, send_b,
-    in_sem, out_sem, xs_send, xs_recv, ys_send, ys_recv, xd_send, xd_recv,
-    yd_send, yd_recv, xx_send, xx_recv, a_send, a_recv, b_send, b_recv,
+    nw, nn, loads, targets, stiff, state, order, s, sens,
+    d, kh, fac_own, fac_in, ys_out, ys_in, yd_out, yd_in, yx_out, yx_in,
+    tile_a, send_a,
+    in_sem, xs_send, xs_recv, ys_send, ys_recv, xd_send, xd_recv,
+    yd_send, yd_recv, xx_send, xx_recv, a_send, a_recv,
 ):
     cells_x, cells_y, depth = stiff.shape
     last = cells_x + 1
@@ -64,14 +64,13 @@
         return at(w, n + steps[side])
 
     barrier = pltpu.get_barrier_semaphore()
-    for m in range(nn):
-        @pl.when(m != n)
-        def _():
-            pl.semaphore_signal(barrier, inc=1, **at(w, jnp.int32(m)))
-    for m in range(nw):
-        @pl.when(m != w)
-        def _():
-            pl.semaphore_signal(barrier, inc=1, **at(jnp.int32(m), n))
+    def greet(k, carry):
+        @pl.when(k != w * nn + n)
+        def _():
+            pl.semaphore_signal(barrier, inc=1, **at(k // nn, k % nn))
+        return carry
+
+    lax.fori_loop(0, nw * nn, greet, 0)
 
     local = [
         pltpu.make_async_copy(stiff, kh.at[pl.ds(1, cells_x)], in_sem.at[0]),
@@ -86,7 +85,7 @@
     act = jnp.where(factor > 0.0, 1.0, 0.0).astype(F32)
     fac_own[...] = jnp.full(fac_own.shape, factor, F32)
 
-    pl.semaphore_wait(barrier, nn - 1 + nw - 1)
+    pl.semaphore_wait(barrier, nw * nn - 1)
 
     edge = (0, cells_x - 1)
     ghost = (0, last)
@@ -296,13 +295,6 @@
     @pl.when(has_y[1])
     def _():
         yx_copy().start()
-
-    results = [
-        pltpu.make_async_copy(s.at[pl.ds(0, 3), pl.ds(1, cells_x)], u_out, out_sem.at[0]),
-        pltpu.make_async_copy(s.at[pl.ds(3, 3), pl.ds(1, cells_x)], l_out, out_sem.at[1]),
-    ]
-    for copy in results:
-        copy.start()
 
     @pl.when(has_y[0])
     def _():
@@ -369,64 +361,45 @@
     send_a[...] = jnp.concatenate(
         [own_row, fold(beside), below, jnp.zeros((5, depth), F32)], axis=0)
 
-    def a_copy(m, slot):
+    me = w * nn + n
+
+    def a_copy(k, slot):
         return pltpu.make_async_remote_copy(
-            src_ref=send_a, dst_ref=tile_a.at[slot], send_sem=a_send.at[m],
-            recv_sem=a_recv.at[slot], **at(w, jnp.int32(m)))
-
-    def b_copy(m, slot):
-        return pltpu.make_async_remote_copy(
-            src_ref=send_b, dst_ref=tile_b.at[slot], send_sem=b_send.at[m],
-            recv_sem=b_recv.at[slot], **at(jnp.int32(m), n))
-
-    for m in range(nn):
-        @pl.when(m != n)
-        def _():
-            a_copy(m, n).start()
-    tile_a[n] = send_a[...]
-    for m in range(nn):
-        @pl.when(m != n)
-        def _():
-            a_copy(m, m).wait_recv()
-
+            src_ref=send_a, dst_ref=tile_a.at[slot], send_sem=a_send.at[k],
+            recv_sem=a_recv.at[slot], **at(k // nn, k % nn))
+
+    def start_a(k, carry):
+        @pl.when(k != me)
+        def _():
+            a_copy(k, me).start()
+        return carry
+
+    lax.fori_loop(0, nw * nn, start_a, 0)
+    tile_a[me] = send_a[...]
+
+    def wait_a(k, carry):
+        @pl.when(k != me)
+        def _():
+            a_copy(k, k).wait_recv()
+        return carry
+
+    lax.fori_loop(0, nw * nn, wait_a, 0)
+
+    wanted = order[me]
     groups_y = nn // 2
-    rows = [zero_row] * (2 * groups_y)
-    for m in range(nn):
-        tile = tile_a[m]
-        rows[m // 2] = rows[m // 2] + tile[0:1]
-        rows[groups_y + m // 2] = rows[groups_y + m // 2] + tile[1:2]
-        if m > 0:
-            rows[(m - 1) // 2] = rows[(m - 1) // 2] + tile[2:3]
-    high = send_b.shape[0]
-    if high > len(rows):
-        rows.append(jnp.zeros((high - len(rows), depth), F32))
-    send_b[...] = jnp.concatenate(rows, axis=0)
-
-    for m in range(nw):
-        @pl.when(m != w)
-        def _():
-            b_copy(m, w).start()
-    tile_b[w] = send_b[...]
-    for m in range(nw):
-        @pl.when(m != w)
-        def _():
-            b_copy(m, m).wait_recv()
-
-    wanted = order[w * nn + n]
-    b_row = lax.broadcasted_iota(jnp.int32, (high, depth), 0)
-    b_block = lax.broadcasted_iota(jnp.int32, (high, depth), 1) // (depth // DZ)
-    picked = jnp.zeros((high, depth), F32)
-    for m in range(nw):
-        near = ((m // 2) * groups_y + b_row) * DZ + b_block
-        far = (((m - 1) // 2) * groups_y + b_row - groups_y) * DZ + b_block if m > 0 else -1
-        index = jnp.where(b_row < groups_y, near, far)
-        index = jnp.where(b_row < 2 * groups_y, index, -1)
-        picked = picked + jnp.where(index == wanted, tile_b[m], 0.0)
+    b_row = lax.broadcasted_iota(jnp.int32, (8, depth), 0)
+    b_block = lax.broadcasted_iota(jnp.int32, (8, depth), 1) // (depth // DZ)
+    picked = jnp.zeros((8, depth), F32)
+    for mw in range(nw):
+        for mn in range(nn):
+            near = ((mw // 2) * groups_y + mn // 2) * DZ
+            beside_x = (((mw - 1) // 2) * groups_y + mn // 2) * DZ if mw > 0 else -DZ
+            beside_y = ((mw // 2) * groups_y + (mn - 1) // 2) * DZ if mn > 0 else -DZ
+            base = jnp.where(b_row == 0, near, jnp.where(b_row == 1, beside_x, beside_y))
+            picked = picked + jnp.where(base + b_block == wanted, tile_a[mw * nn + mn], 0.0)
     scale = math.sqrt(4 * cells_x * cells_y * (depth // DZ))
     sens[0] = jnp.sum(picked) * (-1.0 / scale)
 
-    for copy in results:
-        copy.wait()
     for side in (0, 1):
         @pl.when(has_x[side])
         def _():
@@ -447,35 +420,40 @@
     def _():
         yx_copy().wait_send()
 
-    for m in range(nn):
-        @pl.when(m != n)
-        def _():
-            a_copy(m, n).wait_send()
-    for m in range(nw):
-        @pl.when(m != w)
-        def _():
-            b_copy(m, w).wait_send()
+    def sent_a(k, carry):
+        @pl.when(k != me)
+        def _():
+            a_copy(k, me).wait_send()
+        return carry
+
+    lax.fori_loop(0, nw * nn, sent_a, 0)
+
+
+def write_out(fields, u_out, l_out, sems):
+    cells_x = u_out.shape[1]
+    copies = [
+        pltpu.make_async_copy(fields.at[pl.ds(3 * k, 3), pl.ds(1, cells_x)], out, sems.at[k])
+        for k, out in enumerate((u_out, l_out))
+    ]
+    for copy in copies:
+        copy.start()
+    for copy in copies:
+        copy.wait()
 
 
 def body(nw, nn, loads, targets, stiffness, tile_state, design_order):
     cells_x, cells_y, depth = stiffness.shape
-    high = -(-nn // 8) * 8
     dma = pltpu.SemaphoreType.DMA
     vmem = pltpu.VMEM
     anywhere = pl.BlockSpec(memory_space=pl.ANY)
     smem = pl.BlockSpec(memory_space=pltpu.SMEM)
     field = (6, cells_x + 2, cells_y, depth)
-    return pl.pallas_call(
+    fields, sens = pl.pallas_call(
         functools.partial(kernel, nw, nn),
-        out_shape=(
-            jax.ShapeDtypeStruct(loads.shape, F32),
-            jax.ShapeDtypeStruct(targets.shape, F32),
-            jax.ShapeDtypeStruct((1,), F32),
-        ),
+        out_shape=(pltpu.VMEM(field, F32), jax.ShapeDtypeStruct((1,), F32)),
         in_specs=[anywhere, anywhere, anywhere, smem, smem],
-        out_specs=(anywhere, anywhere, smem),
+        out_specs=(pl.BlockSpec(memory_space=pltpu.VMEM), smem),
         scratch_shapes=[
-            vmem(field, F32),
             vmem(field, F32),
             vmem(field[1:], F32),
             vmem((8, depth), F32),
@@ -486,12 +464,9 @@
             vmem((2, 6, cells_x, depth), F32),
             vmem((6, cells_x, depth), F32),
             vmem((6, cells_x, depth), F32),
-            vmem((nn, 8, depth), F32),
+            vmem((nw * nn, 8, depth), F32),
             vmem((8, depth), F32),
-            vmem((nw, high, depth), F32),
-            vmem((high, depth), F32),
             dma((3,)),
-            dma((2,)),
             dma((2, 4)),
             dma((2, 4)),
             dma((2,)),
@@ -502,15 +477,15 @@
             dma((2,)),
             dma((2,)),
             dma((2,)),
-            dma((nn,)),
-            dma((nn,)),
-            dma((nw,)),
-            dma((nw,)),
+            dma((nw * nn,)),
+            dma((nw * nn,)),
         ],
         compiler_params=pltpu.CompilerParams(
-            collective_id=0, has_side_effects=True, vmem_limit_bytes=40 * 1024 * 1024
+            collective_id=0, has_side_effects=True, vmem_limit_bytes=61440 * 1024
         ),
     )(loads, targets, stiffness, tile_state, design_order)
+    u, l = fields[:3, 1:-1], fields[3:, 1:-1]
+    return u, l, sens
 
 
 def solution(mesh):

time: 45.6 us -> 40.4 us (0.89)
  local copies, waits for them, and re-layouts: 6.79 us -> 1.97 us
    unnamed x10 -> x0, local copies, waits for them, and re-layouts: 6.79 us -> none
    slice x0 -> x1, local copies, waits for them, and re-layouts: none -> 1.97 us  [body(): u, l = (fields[:3, 1:-1], fields[3:, 1:-1])]
where the time goes in v2:
time: 40.4 us; the launch traced here: 40.2 us
  Pallas kernels  35.2 us (87%)
  between operations  3.05 us (8%)
  local copies, waits for them, and re-layouts  1.97 us (5%)
    pallas_call x1, Pallas kernels, body(): pl.pallas_call(functools.partial(kernel, nw, nn), out_shape=(pltpu.VMEM(f...  35.2 us
    slice x1, local copies, waits for them, and re-layouts, body(): u, l = (fields[:3, 1:-1], fields[3:, 1:-1])  1.97 us

profile of v2, /device:TPU:0, one launch (start us, length us, event | category | flops | bytes accessed | tf_op | source)
XLA Modules:
  0.0 40.2 jit_solution(8308578313449475919)
XLA Ops:
  1.3 35.2 %shard_map.76 = (f32[6,34,32,128]{3,2,1,0:T(8,128)S(1)}, f32[1]{0:T(128)}) custom-call(f32[3,32,32,128]{3,2,1,0:T(8,128)} %loads.1, f32[3,32,32,128]{3,2,1,0:T(8,128)} %targets.1, f32[32,32,128]{2,1,0:T(8,128)} %stiff.1, s32[1,1]{1,0:T(1,128)S(6)} %copy.9.state, s32[32]{0:T(128)} %order.1), custom_call_target="tpu_custom_call" | custom-call | tf_op jit(solution)/shard_map/pallas_call | solution.py:451
  36.5 2.0 %fusion = (f32[3,32,32,128]{3,2,1,0:T(8,128)}, f32[3,32,32,128]{3,2,1,0:T(8,128)}) fusion(f32[6,34,32,128]{3,2,1,0:T(8,128)S(1)} %get-tuple-element.5), kind=kLoop, calls=%fused_computation | loop fusion | bytes 6291456 | tf_op jit(solution)/shard_map/slice | solution.py:487

commit v3 on v2

--- a/solution.py
+++ b/solution.py
@@ -241,7 +241,7 @@
         operator(d, yd_in, i, emit_x)
         return carry
 
-    lax.fori_loop(2, cells_x, first_pass, 0)
+    lax.fori_loop(2, cells_x, first_pass, 0, unroll=3)
 
     for side in (0, 1):
         @pl.when(has_x[side])
@@ -262,9 +262,8 @@
         def _():
             kh[ghost[side]] = inner
 
-    lax.fori_loop(0, 2, lambda t, c: first_pass(1 + t * (cells_x - 1), c), 0)
-
-    for side in (0, 1):
+        first_pass(1 + edge[side], 0)
+
         @pl.when(has_x[side])
         def _():
             xd_copy(side).start()
@@ -279,18 +278,17 @@
         def _():
             yd_copy(1 - side).wait_recv()
 
-    lax.fori_loop(2, cells_x, second_pass, 0)
-
-    for side in (0, 1):
+    lax.fori_loop(2, cells_x, second_pass, 0, unroll=3)
+
+    for side in (1, 0):
         @pl.when(has_x[side])
         def _():
             xd_copy(1 - side).wait_recv()
-
-    lax.fori_loop(0, 2, lambda t, c: second_pass(1 + (1 - t) * (cells_x - 1), c), 0)
-
-    @pl.when(has_x[1])
-    def _():
-        xx_copy().start()
+        second_pass(1 + edge[side], 0)
+        if side == 1:
+            @pl.when(has_x[1])
+            def _():
+                xx_copy().start()
 
     @pl.when(has_y[1])
     def _():

time: 40.4 us -> 39.6 us (0.980)
  Pallas kernels: 35.2 us -> 34.4 us
    pallas_call x1, Pallas kernels: 35.2 us -> 34.4 us  [body(): pl.pallas_call(functools.partial(kernel, nw, nn), out_shape=(pltpu.VMEM(f...]
where the time goes in v3:
time: 39.6 us; the launch traced here: 39.4 us
  Pallas kernels  34.4 us (87%)
  between operations  3.05 us (8%)
  local copies, waits for them, and re-layouts  1.97 us (5%)
    pallas_call x1, Pallas kernels, body(): pl.pallas_call(functools.partial(kernel, nw, nn), out_shape=(pltpu.VMEM(f...  34.4 us
    slice x1, local copies, waits for them, and re-layouts, body(): u, l = (fields[:3, 1:-1], fields[3:, 1:-1])  1.97 us

profile of v3, /device:TPU:0, one launch (start us, length us, event | category | flops | bytes accessed | tf_op | source)
XLA Modules:
  0.0 39.4 jit_solution(3647979008103815174)
XLA Ops:
  1.3 34.4 %shard_map.76 = (f32[6,34,32,128]{3,2,1,0:T(8,128)S(1)}, f32[1]{0:T(128)}) custom-call(f32[3,32,32,128]{3,2,1,0:T(8,128)} %loads.1, f32[3,32,32,128]{3,2,1,0:T(8,128)} %targets.1, f32[32,32,128]{2,1,0:T(8,128)} %stiff.1, s32[1,1]{1,0:T(1,128)S(6)} %copy.9.state, s32[32]{0:T(128)} %order.1), custom_call_target="tpu_custom_call" | custom-call | tf_op jit(solution)/shard_map/pallas_call | solution.py:449
  35.7 2.0 %fusion = (f32[3,32,32,128]{3,2,1,0:T(8,128)}, f32[3,32,32,128]{3,2,1,0:T(8,128)}) fusion(f32[6,34,32,128]{3,2,1,0:T(8,128)S(1)} %get-tuple-element.5), kind=kLoop, calls=%fused_computation | loop fusion | bytes 6291456 | tf_op jit(solution)/shard_map/slice | solution.py:485

commit v4 on v3

--- a/solution.py
+++ b/solution.py
@@ -341,7 +341,8 @@
         return own, back, below
 
     start = face_sums(0, (zero_plane, zero_plane, zero_row), behind=False)
-    own, back, below = lax.fori_loop(1, cells_x, face_sums, start)
+    start = face_sums(1, start)
+    own, back, below = lax.fori_loop(2, cells_x, face_sums, start, unroll=3)
 
     @pl.when(has_x[0])
     def _():

time: 39.6 us -> 38.2 us (0.965)
  Pallas kernels: 34.4 us -> 33 us
    pallas_call x1, Pallas kernels: 34.4 us -> 33 us  [body(): pl.pallas_call(functools.partial(kernel, nw, nn), out_shape=(pltpu.VMEM(f...]
where the time goes in v4:
time: 38.2 us; the launch traced here: 38 us
  Pallas kernels  33 us (86%)
  between operations  3.05 us (8%)
  local copies, waits for them, and re-layouts  1.97 us (5%)
    pallas_call x1, Pallas kernels, body(): pl.pallas_call(functools.partial(kernel, nw, nn), out_shape=(pltpu.VMEM(f...  33 us
    slice x1, local copies, waits for them, and re-layouts, body(): u, l = (fields[:3, 1:-1], fields[3:, 1:-1])  1.97 us

profile of v4, /device:TPU:0, one launch (start us, length us, event | category | flops | bytes accessed | tf_op | source)
XLA Modules:
  0.0 38.0 jit_solution(15320750137408478532)
XLA Ops:
  1.3 33.0 %shard_map.76 = (f32[6,34,32,128]{3,2,1,0:T(8,128)S(1)}, f32[1]{0:T(128)}) custom-call(f32[3,32,32,128]{3,2,1,0:T(8,128)} %loads.1, f32[3,32,32,128]{3,2,1,0:T(8,128)} %targets.1, f32[32,32,128]{2,1,0:T(8,128)} %stiff.1, s32[1,1]{1,0:T(1,128)S(6)} %copy.9.state, s32[32]{0:T(128)} %order.1), custom_call_target="tpu_custom_call" | custom-call | tf_op jit(solution)/shard_map/pallas_call | solution.py:450
  34.3 2.0 %fusion = (f32[3,32,32,128]{3,2,1,0:T(8,128)}, f32[3,32,32,128]{3,2,1,0:T(8,128)}) fusion(f32[6,34,32,128]{3,2,1,0:T(8,128)S(1)} %get-tuple-element.5), kind=kLoop, calls=%fused_computation | loop fusion | bytes 6291456 | tf_op jit(solution)/shard_map/slice | solution.py:486
